TPU v7x, 32 devices: a whole 2x2x4 slice. The times are simulated.
32 devices in a mesh: dp: 2 (over z_hi), seq: 8 (over y, x, core), tensor: 2 (over z_lo).
Axes of the slice: x: 2, y: 2, z: 4 (z_hi: 2, z_lo: 2; z = z_hi * 2 + z_lo), core: 2. Of those that a mesh axis runs over, the one named last changes fastest.
Arguments:
- queries: bfloat16 [2, 4096, 4096], P('dp', 'seq', 'tensor'), may hold values from -6 to 6
- keys: bfloat16 [2, 4096, 4096], P('dp', 'seq', 'tensor'), may hold values from -6 to 6
- values: bfloat16 [2, 4096, 4096], P('dp', 'seq', 'tensor'), may hold values from -40 to 40
- grad_out: bfloat16 [2, 4096, 4096], P('dp', 'seq', 'tensor'), may hold values from -48 to 48
- doc_lengths: int32 [2, 4], P('dp'), may hold values from 1 to 3072, 4096 in all within a row
- gain: float32 [4096], P('tensor'), may hold values from 0.1 to 1.9
Outputs:
- layer_out: bfloat16 [2, 4096, 4096], P('dp', 'seq', 'tensor')
- grad_queries: bfloat16 [2, 4096, 4096], P('dp', 'seq', 'tensor')
- grad_keys: bfloat16 [2, 4096, 4096], P('dp', 'seq', 'tensor')
- grad_values: bfloat16 [2, 4096, 4096], P('dp', 'seq', 'tensor')
- grad_gain: float32 [4096], P('tensor')
Inputs may be any that keep to these rules, and one draw needn't show every extreme that they name: `doc_lengths`: each row sums to 4096; in every sequence the longest document has exactly 3072 tokens.
All inputs are finite; a program needn't handle non-finite values.
Results may differ from a plain program's by a relative error of at most 0.0063.
Values may be sent and summed in bfloat16 or wider, within the bound.
A program may use at most 128 MiB of HBM per device.

v0:
```python
import jax
import jax.numpy as jnp
from jax import lax
from jax.sharding import PartitionSpec as P

HEADS = 32
HD = 128


epsilon = 1e-05


def carried(state, lower_bound, upper_bound):
    piece = lax.all_gather(state[None], "seq", axis=0, tiled=True)
    number = jnp.arange(piece.shape[0], dtype=jnp.int32)
    keeping = (number >= lower_bound) & (number < upper_bound)
    return jnp.sum(jnp.where(keeping[:, None, None, None], piece.astype(jnp.float32), 0.0), axis=0)


def head_major(array, shape):
    return jnp.transpose(array.reshape(shape), (1, 0, 2))


def body(queries, keys, values, grad_out, doc_lengths, gain):
    count = queries.shape[1]
    local_width = queries.shape[2]
    local_heads = local_width // HD
    shape = (count, local_heads, HD)
    query = head_major(queries[0], shape)
    key = head_major(keys[0], shape)
    value = head_major(values[0], shape)
    lengths = doc_lengths[0]
    starts = jnp.cumsum(lengths) - lengths
    block = lax.axis_index("seq")
    begin = block * count
    position = begin + jnp.arange(count, dtype=jnp.int32)
    document = jnp.sum((starts[None, :] <= position[:, None]).astype(jnp.int32), axis=1) - 1
    first_doc = document[0]
    last_doc = document[-1]
    numbers = jnp.arange(starts.shape[0], dtype=jnp.int32)
    first_start = jnp.sum(jnp.where(numbers == first_doc, starts, 0))
    last_end = jnp.sum(jnp.where(numbers == last_doc, starts + lengths, 0))
    first_block = first_start // count
    last_block = (last_end - 1) // count
    continues = jnp.logical_not(jnp.any(starts == begin))
    first_mask = (document == first_doc) & continues
    last_mask = document == last_doc
    indices = jnp.arange(count, dtype=jnp.int32)
    same = (indices[:, None] >= indices[None, :]) & (document[:, None] == document[None, :])
    key_last = jnp.where(last_mask[None, :, None], key, 0)
    value_last = jnp.where(last_mask[None, :, None], value, 0)
    query_first = jnp.where(first_mask[None, :, None], query, 0)
    state = jnp.einsum("htd,hte->hde", key_last, value, preferred_element_type=jnp.float32).astype(
        jnp.bfloat16
    )
    incoming = carried(state, first_block, block)
    carry_in = jnp.where(continues, incoming, 0.0).astype(jnp.bfloat16)
    scores = jnp.einsum("htd,hsd->hts", query, key, preferred_element_type=jnp.float32)
    scores = jnp.where(same[None], scores, 0.0).astype(jnp.bfloat16)
    attended = jnp.einsum("hts,hsd->htd", scores, value, preferred_element_type=jnp.float32)
    attended = attended + jnp.einsum(
        "htd,hde->hte", query_first, carry_in, preferred_element_type=jnp.float32
    )
    attended = jnp.transpose(attended, (1, 0, 2)).reshape(count, local_width)
    squares = lax.psum(jnp.sum(attended * attended, axis=1), "tensor")
    rscale = lax.rsqrt(squares / (HEADS * HD) + epsilon)
    unit = attended * rscale[:, None]
    layer_out = (gain * unit).astype(jnp.bfloat16)
    upstream = grad_out[0].astype(jnp.float32)
    scaled = upstream * gain
    inner = lax.psum(jnp.sum(scaled * unit, axis=1), "tensor") / (HEADS * HD)
    grad_gain = lax.psum(jnp.sum(upstream * unit, axis=0), ("dp", "seq"))
    d_att = head_major(
        (rscale[:, None] * (scaled - unit * inner[:, None])).astype(jnp.bfloat16), shape
    )
    d_first = jnp.where(first_mask[None, :, None], d_att, 0)
    back_state = jnp.einsum(
        "htd,hte->hde", query_first, d_att, preferred_element_type=jnp.float32
    ).astype(jnp.bfloat16)
    outgoing = carried(back_state, block + 1, last_block + 1)
    carry_back = jnp.where(last_block > block, outgoing, 0.0).astype(jnp.bfloat16)
    d_scores = jnp.einsum("hte,hse->hts", d_att, value, preferred_element_type=jnp.float32)
    d_scores = jnp.where(same[None], d_scores, 0.0).astype(jnp.bfloat16)
    grad_query = jnp.einsum("hts,hsd->htd", d_scores, key, preferred_element_type=jnp.float32)
    grad_query = grad_query + jnp.einsum(
        "hte,hde->htd", d_first, carry_in, preferred_element_type=jnp.float32
    )
    grad_key = jnp.einsum("hts,htd->hsd", d_scores, query, preferred_element_type=jnp.float32)
    grad_key = grad_key + jnp.einsum(
        "hse,hde->hsd", value_last, carry_back, preferred_element_type=jnp.float32
    )
    grad_value = jnp.einsum("hts,hte->hse", scores, d_att, preferred_element_type=jnp.float32)
    grad_value = grad_value + jnp.einsum(
        "hsd,hde->hse", key_last, carry_back, preferred_element_type=jnp.float32
    )
    out_shape = (1, count, local_width)

    def token_major(array):
        return jnp.transpose(array.astype(jnp.bfloat16), (1, 0, 2)).reshape(out_shape)

    return (
        layer_out.reshape(out_shape),
        token_major(grad_query),
        token_major(grad_key),
        token_major(grad_value),
        grad_gain,
    )


def solution(mesh):
    in_specs = (
        P("dp", "seq", "tensor"),
        P("dp", "seq", "tensor"),
        P("dp", "seq", "tensor"),
        P("dp", "seq", "tensor"),
        P("dp", None),
        P("tensor"),
    )
    out_specs = (
        P("dp", "seq", "tensor"),
        P("dp", "seq", "tensor"),
        P("dp", "seq", "tensor"),
        P("dp", "seq", "tensor"),
        P("tensor"),
    )
    return jax.shard_map(body, mesh=mesh, in_specs=in_specs, out_specs=out_specs, check_vma=False)
```

profile of v0, /device:TPU:0, one launch (start us, length us, event | category | flops | bytes accessed | tf_op | source)
XLA Modules:
  0.0 192.1 jit_solution(6425590472065875236)
XLA Ops:
  11.3 3.9 %copy.54 = bf16[1,512,2048]{1,2,0:T(8,128)(2,1)} copy(bf16[1,512,2048]{2,1,0:T(8,128)(2,1)} %param.7) | data formatting | bytes 4194304 | tf_op args[1]
  29.8 4.2 %copy.62 = f32[1,512,2048]{1,2,0:T(8,128)} copy(bf16[1,512,2048]{2,1,0:T(8,128)(2,1)} %param.9) | data formatting | bytes 6291456 | tf_op jit(solution)/shard_map/convert_element_type | solution.py:69
  34.2 4.2 %select_convert_fusion.1 = bf16[16,512,512]{2,1,0:T(8,128)(2,1)S(1)} fusion(bf16[16,512,128]{1,2,0:T(8,128)(2,1)S(1)} %bitcast.92, bf16[16,512,128]{1,2,0:T(8,128)(2,1)} %bitcast.101, pred[512,512]{1,0:T(8,128)(4,1)S(1)} %fusion.26), kind=kOutput, calls=%fused_computation.1 | convolution fusion | flops 1082130432 | bytes 12845056 | tf_op jit(solution)/shard_map/htd,hsd->hts/dot_general | solution.py:58
  41.6 4.7 %fusion.41 = f32[16,512,128]{1,2,0:T(8,128)} fusion(bf16[16,512,512]{2,1,0:T(8,128)(2,1)S(1)} %select_convert_fusion.1, bf16[16,512,128]{1,2,0:T(8,128)(2,1)S(1)} %bitcast.98), kind=kOutput, calls=%fused_computation.73 | convolution fusion | flops 1073741824 | bytes 14680064 | tf_op jit(solution)/shard_map/hts,hsd->htd/dot_general | solution.py:60
  46.4 15.9 %all-gather.5.cloned.1.call-done = bf16[128,128,128]{2,1,0:T(8,128)(2,1)} async-done(((bf16[16,128,128]{2,1,0:T(8,128)(2,1)}), bf16[128,128,128]{2,1,0:T(8,128)(2,1)}) %all-gather.5.cloned.1.call-update) | async-done | bytes 4194320 | tf_op jit(solution)/shard_map/all_gather | solution.py:14
  62.2 3.3 %fusion.1 = bf16[16,128,128]{2,1,0:T(8,128)(2,1)S(1)} fusion(bf16[8,16,128,128]{3,2,1,0:T(8,128)(2,1)} %bitcast.109, pred[8]{0:T(512)(128)(4,1)S(1)} %compare_and_fusion.1), kind=kLoop, calls=%fused_computation.5 | loop fusion | flops 6029312 | bytes 4718600 | tf_op jit(solution)/shard_map/reduce_sum | solution.py:17
  68.5 5.4 %copy.63 = f32[512,2048]{1,0:T(8,128)} copy(f32[512,2048]{0,1:T(8,128)} %bitcast.90) | data formatting | bytes 8388608 | tf_op jit(solution)/shard_map/reshape | solution.py:64
  73.8 4.9 %psum.21 = f32[512]{0:T(512)S(1)} all-reduce(f32[512]{0:T(512)S(1)} %get-tuple-element.28), channel_id=1, replica_groups=mesh['dp'=2,'seq'=8,'tensor'=2] {'tensor'}, use_global_device_ids=true, to_apply=%region_6.7 | all-reduce | flops 512 | bytes 4096 | tf_op jit(solution)/shard_map/psum | solution.py:65
  78.8 4.0 %fusion.4 = (f32[2048]{0:T(1024)S(1)}, f32[512]{0:T(512)S(1)}) fusion(f32[512,2048]{1,0:T(8,128)} %copy.63, bf16[1,512,2048]{2,1,0:T(8,128)(2,1)} %param.9, f32[512]{0:T(512)S(1)} %add_rsqrt_fusion, f32[2048]{0:T(1024)S(1)} %copy-done.11), kind=kLoop, calls=%fused_computation.10 | loop fusion | flops 7337472 | bytes 6311936 | tf_op jit(solution)/shard_map/reduce_sum | solution.py:72
  82.8 5.1 %psum.22 = f32[512]{0:T(512)S(1)} all-reduce(f32[512]{0:T(512)S(1)} %get-tuple-element.21), channel_id=1, replica_groups=mesh['dp'=2,'seq'=8,'tensor'=2] {'tensor'}, use_global_device_ids=true, to_apply=%region_8.9 | all-reduce | flops 512 | bytes 4096 | tf_op jit(solution)/shard_map/psum | solution.py:71
  87.9 4.2 %fusion.10 = bf16[16,512,128]{1,2,0:T(8,128)(2,1)S(1)} fusion(f32[16,512,128]{1,2,0:T(8,128)} %get-tuple-element.29, f32[512,16,128]{0,2,1:T(8,128)} %bitcast.104, f32[512]{0:T(512)S(1)} %broadcast_multiply_fusion, f32[16,128]{1,0:T(8,128)S(1)} %bitcast.110, f32[512]{0:T(512)S(1)} %add_rsqrt_fusion), kind=kLoop, calls=%fused_computation.23 | loop fusion | flops 6291456 | bytes 10498048 | tf_op jit(solution)/shard_map/transpose | solution.py:21
  95.8 4.8 %select_convert_fusion = bf16[16,512,512]{2,1,0:T(8,128)(2,1)S(1)} fusion(bf16[16,512,128]{1,2,0:T(8,128)(2,1)} %copy-done.7, bf16[16,512,128]{1,2,0:T(8,128)(2,1)} %bitcast.97, pred[512,512]{1,0:T(8,128)(4,1)S(1)} %fusion.26), kind=kOutput, calls=%fused_computation | convolution fusion | flops 1082130432 | bytes 12845056 | tf_op jit(solution)/shard_map/hte,hse->hts/dot_general | solution.py:82
  100.7 4.8 %fusion.42 = f32[16,512,128]{1,2,0:T(8,128)} fusion(bf16[16,512,512]{2,1,0:T(8,128)(2,1)S(1)} %select_convert_fusion, bf16[16,512,128]{1,2,0:T(8,128)(2,1)S(1)} %bitcast.102), kind=kOutput, calls=%fused_computation.74 | convolution fusion | flops 1073741824 | bytes 14680064 | tf_op jit(solution)/shard_map/hts,hsd->htd/dot_general | solution.py:84
  105.7 4.3 %add_convert_fusion.2 = bf16[16,512,128]{1,2,0:T(8,128)(2,1)} fusion(f32[16,512,128]{1,2,0:T(8,128)} %fusion.42, bf16[16,512,128]{1,2,0:T(8,128)(2,1)S(1)} %copy-done.8, pred[512]{0:T(512)(128)(4,1)S(1)} %get-tuple-element.25, bf16[16,128,128]{2,1,0:T(8,128)(2,1)S(1)} %fusion.1, pred[]{:T(512)S(6)} %not.3), kind=kOutput, calls=%fused_computation.20 | convolution fusion | flops 271843328 | bytes 8913409 | tf_op jit(solution)/shard_map/hte,hde->htd/dot_general | solution.py:85
  109.9 3.9 %copy.71 = bf16[1,512,2048]{2,1,0:T(8,128)(2,1)} copy(bf16[1,512,2048]{1,2,0:T(8,128)(2,1)} %bitcast.106) | data formatting | bytes 4194304
  113.8 5.5 %copy.61 = f32[1,512,2048]{2,1,0:T(8,128)} copy(f32[1,512,2048]{1,2,0:T(8,128)} %bitcast.91) | data formatting | bytes 8388608 | tf_op jit(solution)/shard_map/reshape | solution.py:64
  119.3 32.1 %psum.23 = f32[2048]{0:T(1024)} all-reduce(f32[2048]{0:T(1024)S(1)} %get-tuple-element.20), channel_id=1, replica_groups=mesh['dp'=2,'seq'=8,'tensor'=2] {'dp','seq'}, use_global_device_ids=true, to_apply=%region_12.13 | all-reduce | flops 2048 | bytes 16384 | tf_op jit(solution)/shard_map/psum | solution.py:72
  151.4 3.9 %multiply_convert_fusion = bf16[1,512,2048]{2,1,0:T(8,128)(2,1)} fusion(f32[1,512,2048]{2,1,0:T(8,128)} %copy.61, f32[512]{0:T(512)S(1)} %add_rsqrt_fusion, f32[2048]{0:T(1024)S(1)} %copy-done.11), kind=kLoop, calls=%fused_computation.21 | loop fusion | flops 3145728 | bytes 6301696 | tf_op jit(solution)/shard_map/convert_element_type | solution.py:68
  155.4 6.6 %fusion.43 = f32[16,512,128]{1,2,0:T(8,128)} fusion(bf16[16,512,128]{1,2,0:T(8,128)(2,1)S(1)} %bitcast.95, bf16[16,512,512]{2,1,0:T(8,128)(2,1)} %copy-done), kind=kOutput, calls=%fused_computation.75 | convolution fusion | flops 1073741824 | bytes 14680064 | tf_op jit(solution)/shard_map/hts,htd->hsd/dot_general | solution.py:88
  161.9 3.3 %fusion = bf16[16,128,128]{2,1,0:T(8,128)(2,1)S(1)} fusion(bf16[8,16,128,128]{3,2,1,0:T(8,128)(2,1)} %bitcast.108, pred[8]{0:T(512)(128)(4,1)S(1)} %compare_and_fusion), kind=kLoop, calls=%fused_computation.3 | loop fusion | flops 6029312 | bytes 4718600 | tf_op jit(solution)/shard_map/reduce_sum | solution.py:17
  166.8 6.2 %add_convert_fusion = bf16[16,512,128]{1,2,0:T(8,128)(2,1)} fusion(f32[16,512,128]{1,2,0:T(8,128)S(1)} %fusion.16, bf16[16,512,128]{1,2,0:T(8,128)(2,1)S(1)} %copy-done.9, bf16[16,512,512]{2,1,0:T(8,128)(2,1)} %copy-done.1), kind=kOutput, calls=%fused_computation.18 | convolution fusion | flops 1075838976 | bytes 16777216 | tf_op jit(solution)/shard_map/hts,hte->hse/dot_general | solution.py:92
  173.0 4.1 %copy.73 = bf16[1,512,2048]{2,1,0:T(8,128)(2,1)} copy(bf16[1,512,2048]{1,2,0:T(8,128)(2,1)} %bitcast.107) | data formatting | bytes 4194304
  177.1 4.2 %add_convert_fusion.1 = bf16[16,512,128]{1,2,0:T(8,128)(2,1)} fusion(f32[16,512,128]{1,2,0:T(8,128)} %fusion.43, bf16[16,512,128]{1,2,0:T(8,128)(2,1)S(1)} %bitcast.99, pred[512]{0:T(512)(128)(4,1)S(1)} %get-tuple-element.24, bf16[16,128,128]{2,1,0:T(8,128)(2,1)S(1)} %fusion, pred[]{:T(512)S(6)} %gt.3), kind=kOutput, calls=%fused_computation.19 | convolution fusion | flops 271843328 | bytes 8913409 | tf_op jit(solution)/shard_map/hse,hde->hsd/dot_general | solution.py:89
  181.3 3.9 %copy.72 = bf16[1,512,2048]{2,1,0:T(8,128)(2,1)} copy(bf16[1,512,2048]{1,2,0:T(8,128)(2,1)} %bitcast.105) | data formatting | bytes 4194304
  (51 shorter events, 26.8 us)
Async XLA Ops:
  7.2 55.1 %all-gather.5.cloned.1.call-start = ((), (), s32[]{:S(2)}) async-start(), calls=%async_computation | async-start | bytes 4718592 | tf_op jit(solution)/shard_map/all_gather | solution.py:14
  18.1 4.5 %copy-start.2 = (bf16[1,512,2048]{1,2,0:T(8,128)(2,1)}, bf16[1,512,2048]{1,2,0:T(8,128)(2,1)S(1)}, u32[]{:S(2)}) copy-start(bf16[1,512,2048]{1,2,0:T(8,128)(2,1)S(1)} %copy.57) | copy-start | bytes 6291460
  19.5 3.2 %copy-start.12 = (s32[1,4]{1,0:T(1,128)S(1)}, s32[1,4]{1,0:T(1,128)}, u32[]{:S(2)}) copy-start(s32[1,4]{1,0:T(1,128)} %param.10) | copy-start | bytes 52
  22.7 139.3 %all-gather.7.cloned.1.call-start = ((), (), s32[]{:S(2)}) async-start(), calls=%async_computation.1 | async-start | bytes 4718592 | tf_op jit(solution)/shard_map/all_gather | solution.py:14
  34.2 7.4 %copy-start.3 = (bf16[1,512,2048]{1,2,0:T(8,128)(2,1)S(1)}, bf16[1,512,2048]{1,2,0:T(8,128)(2,1)}, u32[]{:S(2)}) copy-start(bf16[1,512,2048]{1,2,0:T(8,128)(2,1)} %copy-done.2) | copy-start | bytes 6291460
  38.4 3.2 %copy-start.1 = (bf16[16,512,512]{2,1,0:T(8,128)(2,1)}, bf16[16,512,512]{2,1,0:T(8,128)(2,1)S(1)}, u32[]{:S(2)}) copy-start(bf16[16,512,512]{2,1,0:T(8,128)(2,1)S(1)} %select_convert_fusion.1) | copy-start | bytes 25165828
  62.2 3.4 %copy-start.10 = (f32[16,512,128]{1,2,0:T(8,128)S(1)}, f32[16,512,128]{1,2,0:T(8,128)}, u32[]{:S(2)}) copy-start(f32[16,512,128]{1,2,0:T(8,128)} %fusion.41) | copy-start | bytes 12582916
  68.4 10.3 %copy-start.11 = (f32[2048]{0:T(1024)S(1)}, f32[2048]{0:T(1024)}, u32[]{:S(2)}) copy-start(f32[2048]{0:T(1024)} %param.11) | copy-start | bytes 24580
  92.2 1.4 copy-start.7
  95.8 4.8 %copy-start.5 = (bf16[1,512,2048]{1,2,0:T(8,128)(2,1)S(1)}, bf16[1,512,2048]{1,2,0:T(8,128)(2,1)}, u32[]{:S(2)}) copy-start(bf16[1,512,2048]{1,2,0:T(8,128)(2,1)} %copy.54) | copy-start | bytes 6291460
  100.6 5.0 %copy-start = (bf16[16,512,512]{2,1,0:T(8,128)(2,1)}, bf16[16,512,512]{2,1,0:T(8,128)(2,1)S(1)}, u32[]{:S(2)}) copy-start(bf16[16,512,512]{2,1,0:T(8,128)(2,1)S(1)} %select_convert_fusion) | copy-start | bytes 25165828
  100.6 5.0 %copy-start.8 = (bf16[16,512,128]{1,2,0:T(8,128)(2,1)S(1)}, bf16[16,512,128]{1,2,0:T(8,128)(2,1)}, u32[]{:S(2)}) copy-start(bf16[16,512,128]{1,2,0:T(8,128)(2,1)} %copy-done.7) | copy-start | bytes 6291460
  161.9 3.3 %copy-start.6 = (bf16[1,512,2048]{1,2,0:T(8,128)(2,1)S(1)}, bf16[1,512,2048]{1,2,0:T(8,128)(2,1)}, u32[]{:S(2)}) copy-start(bf16[1,512,2048]{1,2,0:T(8,128)(2,1)} %copy.54) | copy-start | bytes 6291460
  165.2 1.6 copy-start.9
  173.0 4.1 %copy-start.4 = (bf16[1,512,2048]{1,2,0:T(8,128)(2,1)S(1)}, bf16[1,512,2048]{1,2,0:T(8,128)(2,1)}, u32[]{:S(2)}) copy-start(bf16[1,512,2048]{1,2,0:T(8,128)(2,1)} %copy-done.2) | copy-start | bytes 6291460
Sparse Core Ops, SparseCore 0:
  22.8 39.4 all-gather.4
  95.3 37.0 all-gather.6
where the time goes:
time: 193 us; the launch traced here: 192 us
  matrix products  48 us (25%)
  local copies, waits for them, and re-layouts  42.9 us (22%)
  blocking collectives  42.2 us (22%)
  other arithmetic  25.2 us (13%)
  between operations  17.8 us (9%)
  waiting for transfers between devices  15.9 us (8%)
    psum x1, blocking collectives, body(): grad_gain = lax.psum(jnp.sum(upstream * unit, axis=0), ('dp', 'seq'))  32.1 us
    unnamed x32, local copies, waits for them, and re-layouts  27.3 us
    all_gather x2, waiting for transfers between devices, carried(): piece = lax.all_gather(state[None], 'seq', axis=0, tiled=True)  15.9 us
    reshape x2, local copies, waits for them, and re-layouts, body(): attended = jnp.transpose(attended, (1, 0, 2)).reshape(count, local_width)  10.8 us
    dot_general x1, matrix products, body(): jnp.einsum('hts,htd->hsd', d_scores, query, preferred_element_type=jnp.fl...  6.56 us
    reduce_sum x2, other arithmetic, carried(): jnp.sum(jnp.where(keeping[:, None, None, None], piece.astype(jnp.float32)...  6.56 us
    dot_general x1, matrix products, body(): jnp.einsum('hts,hte->hse', scores, d_att, preferred_element_type=jnp.floa...  6.23 us
    psum x1, blocking collectives, body(): inner = lax.psum(jnp.sum(scaled * unit, axis=1), 'tensor') / (HEADS * HD)  5.12 us
  transfers between devices with their start and end apart: 2, of which 1 were waited for; matrix products, arithmetic and copies ran while one was open for 27% of the time, Pallas kernels for 0%

commit v1 on v0

v1 whole, which is shorter than its diff:
```python
import functools

import jax
import jax.numpy as jnp
from jax import lax
from jax.experimental import pallas as pl
from jax.experimental.pallas import tpu as pltpu
from jax.sharding import PartitionSpec as P

HD = 128
CHUNK = 2
EPSILON = 1e-05
MESH = pl.DeviceIdType.MESH
F32 = jnp.float32
BF16 = jnp.bfloat16


def nn(a, b):
    return lax.dot_general(a, b, (((1,), (0,)), ((), ())), preferred_element_type=F32)


def nt(a, b):
    return lax.dot_general(a, b, (((1,), (1,)), ((), ())), preferred_element_type=F32)


def tn(a, b):
    return lax.dot_general(a, b, (((0,), (0,)), ((), ())), preferred_element_type=F32)


def cols(h):
    return pl.ds(pl.multiple_of(h * HD, HD), HD)


def bits_of(n):
    return n.bit_length() - 1


def kernel(
    sizes, len_ref, q_hbm, k_hbm, v_hbm, g_hbm, gain_ref,
    lo_hbm, gq_hbm, gk_hbm, gv_hbm, gg_ref,
    q, k, v, g, att, gvp, scr, dat, lo, gq, gk, gv, mask, fmf, lmf, fmb, lmb,
    acc, rs, qs, st, sr, sa, rr, pacc, pf, pr, ci, ts, tr, gs, gr,
    in_sem, out_sem, ssem, rsem,
):
    n_dp, n_seq, n_tensor, docs = sizes
    T, W = q.shape
    H = W // HD
    half = H // 2
    C = half // CHUNK
    J = bits_of(n_seq) - 1
    T2 = T // 2
    per = (3 + J) * C
    tensor_base = 2 * per
    gain_base = tensor_base + bits_of(n_tensor)

    loads = [
        pltpu.make_async_copy(src, dst, in_sem.at[i])
        for i, (src, dst) in enumerate(((k_hbm, k), (v_hbm, v), (q_hbm, q), (g_hbm, g)))
    ]
    for load in loads:
        load.start()

    me = lax.axis_index("seq")
    dp = lax.axis_index("dp")
    ten = lax.axis_index("tensor")

    def flip(index, j):
        bit = lax.rem(lax.div(index, 1 << j), 2)
        return index + (1 - 2 * bit) * (1 << j)

    seq_peers = [{"seq": flip(me, j)} for j in range(J + 1)]
    dp_peers = [{"dp": flip(dp, j)} for j in range(bits_of(n_dp))]
    tensor_peers = [{"tensor": flip(ten, j)} for j in range(bits_of(n_tensor))]
    peers = seq_peers + dp_peers + tensor_peers
    barrier = pltpu.get_barrier_semaphore()
    for peer in peers:
        pl.semaphore_signal(barrier, inc=1, device_id=peer, device_id_type=MESH)

    core = lax.rem(me, 2)
    mine = core * half
    other = (1 - core) * half
    begin = me * T

    starts = []
    run = jnp.int32(0)
    for d in range(docs):
        starts.append(run)
        run = run + len_ref[0, d]
    ends = starts[1:] + [run]

    def first_start(pos):
        best = jnp.int32(0)
        for s in starts:
            best = jnp.maximum(best, jnp.where(s <= pos, s, 0))
        return best

    def last_end(pos):
        best = run
        for e in ends:
            best = jnp.minimum(best, jnp.where(e > pos, e, run))
        return best

    def flag(cond):
        return jnp.where(cond, 1.0, 0.0).astype(F32)

    bit_of = [lax.rem(lax.div(me, 1 << j), 2) for j in range(J + 1)]
    fwd, bwd = [], []
    chip = (me - core) * T
    for j in range(J + 1):
        size = 2 << j
        low = lax.div(me, size) * size
        mid = (low + (1 << j)) * T
        high = (low + size) * T
        wf = flag(first_start(high) < mid)
        wb = flag(last_end(low * T - 1) > mid)
        right = flag(bit_of[j] == 1)
        left = 1.0 - right
        fwd.append((
            right + left * wf, left + right * wf,
            right * flag(first_start(chip) < mid),
        ))
        bwd.append((
            left + right * wb, right + left * wb,
            left * flag(last_end(chip + 2 * T - 1) > mid),
        ))
    is_one = flag(core == 1)
    is_zero = 1.0 - is_one
    f_state = is_one * flag(first_start(begin) < begin)
    f_pre = is_zero + is_one * flag(first_start(begin) < chip)
    b_state = is_zero * flag(last_end(begin + T - 1) > begin + T)
    b_pre = is_one + is_zero * flag(last_end(begin + T - 1) > chip + 2 * T)

    row = lax.broadcasted_iota(jnp.int32, (T, HD), 0) + begin
    own_start = first_start(begin)
    keep_first = (row < last_end(begin)) & (own_start < begin)
    keep_last = row >= first_start(begin + T - 1)
    fm = jnp.where(keep_first, 1.0, 0.0).astype(F32)
    lm = jnp.where(keep_last, 1.0, 0.0).astype(F32)
    fmf[...] = fm
    lmf[...] = lm
    fmb[...] = fm.astype(BF16)
    lmb[...] = lm.astype(BF16)
    for r in range(T // HD):
        t_pos = lax.broadcasted_iota(jnp.int32, (HD, T), 0) + (begin + r * HD)
        s_pos = lax.broadcasted_iota(jnp.int32, (HD, T), 1) + begin
        t_start = jnp.zeros((HD, T), jnp.int32)
        for s in starts:
            t_start = jnp.maximum(t_start, jnp.where(t_pos >= s, s, 0))
        inside = (s_pos <= t_pos) & (s_pos >= t_start)
        mask[r * HD:(r + 1) * HD, :] = jnp.where(inside, 1.0, 0.0).astype(F32)

    def remote(src, dst, index, peer):
        return pltpu.make_async_remote_copy(
            src_ref=src, dst_ref=dst, send_sem=ssem.at[index], recv_sem=rsem.at[index],
            device_id=peer, device_id_type=MESH,
        )

    def chunk(c):
        return pl.ds(c * CHUNK, CHUNK)

    def state_copy(w, cc):
        return remote(st.at[w, chunk(cc)], sr.at[w, chunk(cc)], w * per + cc, seq_peers[0])

    def step_copy(w, j, c):
        return remote(
            sa.at[w, j, chunk(c)], rr.at[w, j, chunk(c)],
            w * per + (2 + j) * C + c, seq_peers[j + 1],
        )

    def final_copy(w, c):
        return remote(pf.at[w, chunk(c)], pr.at[w, chunk(c)], w * per + (2 + J) * C + c, seq_peers[0])

    def begin_step(w, coef, c):
        cc = core * C + c
        state_copy(w, cc).wait_recv()
        own, theirs = st[w, chunk(cc)].astype(F32), sr[w, chunk(cc)].astype(F32)
        sa[w, 0, chunk(c)] = (coef[0][0] * own + coef[0][1] * theirs).astype(BF16)
        step_copy(w, 0, c).start()

    def step(w, coef, j, c):
        step_copy(w, j, c).wait_recv()
        got = rr[w, j, chunk(c)].astype(F32)
        keep = coef[j + 1]
        total = keep[2] * got
        if j > 0:
            total = total + pacc[chunk(c)]
        if j < J - 1:
            pacc[chunk(c)] = total
            new = keep[0] * sa[w, j, chunk(c)].astype(F32) + keep[1] * got
            sa[w, j + 1, chunk(c)] = new.astype(BF16)
            step_copy(w, j + 1, c).start()
        else:
            pf[w, chunk(c)] = total.astype(BF16)
            final_copy(w, c).start()

    def interleave(w, coef, work, before, extra):
        order = sorted(
            [(c + j, -j, c) for j in range(J) for c in range(C)]
        )
        events = [functools.partial(begin_step, w, coef, c) for c in range(C)]
        first = len(events)
        events += [functools.partial(step, w, coef, -mj, c) for _, mj, c in order]
        done = 0

        def to(upto):
            nonlocal done
            if upto > done:
                lax.fori_loop(done, upto, lambda h, x: (work(h), x)[1], 0)
                done = upto

        to(before)
        later = len(events) - first
        for i, event in enumerate(events):
            if i >= first:
                to(before + ((H - before) * (i - first + 1)) // later)
            event()
            if extra and i >= first and (i - first) % 2 == 1:
                extra.pop(0)()
        to(H)
        while extra:
            extra.pop(0)()

    loads[0].wait()
    loads[1].wait()
    pl.semaphore_wait(barrier, len(peers))

    def state_chunk(i, x):
        for u in range(CHUNK):
            h = lax.rem(other + i * CHUNK + u, H)
            st[0, h] = tn(k[:, cols(h)] * lmb[...], v[:, cols(h)]).astype(BF16)
        state_copy(0, lax.rem((1 - core) * C + i, 2 * C)).start()
        return x

    lax.fori_loop(0, 2 * C, state_chunk, 0)
    loads[2].wait()

    def local_forward(h):
        qh, kh, vh = q[:, cols(h)], k[:, cols(h)], v[:, cols(h)]
        top = (nt(qh[:T2], kh[:T2]) * mask[:T2, :T2]).astype(BF16)
        low = (nt(qh[T2:], kh) * mask[T2:, :]).astype(BF16)
        scr[h, :T2, :T2] = top
        scr[h, T2:, :] = low
        att[:T2, cols(h)] = nn(top, vh[:T2])
        att[T2:, cols(h)] = nn(low, vh)

    interleave(0, fwd, local_forward, 2, [])
    loads[3].wait()
    acc[...] = jnp.zeros_like(acc)

    def finish_forward(h, pre):
        carry = (f_state * sr[0, h].astype(F32) + f_pre * pre.astype(F32)).astype(BF16)
        ci[h] = carry
        x = att[:, cols(h)] + fmf[...] * nn(q[:, cols(h)], carry)
        att[:, cols(h)] = x
        acc[0] += x * x
        acc[1] += (g[:, cols(h)].astype(F32) * gain_ref[pl.ds(h, 1), :]) * x

    def forward_mine(i, x):
        finish_forward(mine + i, pf[0, i])
        return x

    lax.fori_loop(0, half, forward_mine, 0)

    def forward_other(c, x):
        state_copy(0, (1 - core) * C + c).wait_recv()
        final_copy(0, c).wait_recv()
        for u in range(CHUNK):
            finish_forward(other + c * CHUNK + u, pr[0, c * CHUNK + u])
        return x

    lax.fori_loop(0, C, forward_other, 0)

    squares = jnp.sum(acc[0].T, axis=0, keepdims=True)
    inners = jnp.sum(acc[1].T, axis=0, keepdims=True)
    which = lax.broadcasted_iota(jnp.int32, (8, T), 0)
    sums = jnp.where(which < 4, squares, inners)
    for j, peer in enumerate(tensor_peers):
        ts[j] = sums
        swap = remote(ts.at[j], tr.at[j], tensor_base + j, peer)
        swap.start()
        swap.wait()
        sums = sums + tr[j]
    width = W * n_tensor
    rscale = lax.rsqrt(sums[0:1] / width + EPSILON)
    inner = rscale * sums[4:5] / width
    rs[...] = jnp.broadcast_to(rscale, (HD, T)).T
    qs[...] = jnp.broadcast_to(rscale * rscale * inner, (HD, T)).T

    def back_chunk(i, x):
        for u in range(CHUNK):
            h = lax.rem(other + i * CHUNK + u, H)
            a = att[:, cols(h)]
            up = g[:, cols(h)].astype(F32)
            gain = gain_ref[pl.ds(h, 1), :]
            unit = a * rs[...]
            lo[:, cols(h)] = (gain * unit).astype(BF16)
            gs[0, pl.ds(h, 1), :] = jnp.sum(up * unit, axis=0, keepdims=True)
            d = (rs[...] * (up * gain) - qs[...] * a).astype(BF16)
            dat[:, cols(h)] = d
            st[1, h] = tn(q[:, cols(h)] * fmb[...], d).astype(BF16)
        state_copy(1, lax.rem((1 - core) * C + i, 2 * C)).start()
        return x

    lax.fori_loop(0, 2 * C, back_chunk, 0)
    out_lo = pltpu.make_async_copy(lo, lo_hbm, out_sem.at[3 * H])
    out_lo.start()

    gain_peers = dp_peers + seq_peers[::-1]

    def gain_copy(j):
        return remote(gs.at[j], gr.at[j], gain_base + j, gain_peers[j])

    gain_copy(0).start()

    def gain_step(j):
        gain_copy(j).wait_recv()
        total = gs[j] + gr[j]
        if j + 1 < len(gain_peers):
            gs[j + 1] = total
            gain_copy(j + 1).start()
        else:
            gg_ref[...] = total

    def out_copy(n, src, dst, h):
        return pltpu.make_async_copy(src.at[:, cols(h)], dst.at[:, cols(h)], out_sem.at[n * H + h])

    def local_backward(h):
        qh, kh, vh, dh = q[:, cols(h)], k[:, cols(h)], v[:, cols(h)], dat[:, cols(h)]
        top = (nt(dh[:T2], vh[:T2]) * mask[:T2, :T2]).astype(BF16)
        low = (nt(dh[T2:], vh) * mask[T2:, :]).astype(BF16)
        into = nt(dh, ci[h]) * fmf[...]
        gq[:T2, cols(h)] = (nn(top, kh[:T2]) + into[:T2]).astype(BF16)
        gq[T2:, cols(h)] = (nn(low, kh) + into[T2:]).astype(BF16)
        out_copy(0, gq, gq_hbm, h).start()
        att[:T2, cols(h)] = tn(top, qh[:T2]) + tn(low[:, :T2], qh[T2:])
        att[T2:, cols(h)] = tn(low[:, T2:], qh[T2:])
        stop, slow = scr[h, :T2, :T2], scr[h, T2:, :]
        gvp[:T2, cols(h)] = tn(stop, dh[:T2]) + tn(slow[:, :T2], dh[T2:])
        gvp[T2:, cols(h)] = tn(slow[:, T2:], dh[T2:])

    interleave(
        1, bwd, local_backward, 4,
        [functools.partial(gain_step, j) for j in range(len(gain_peers))],
    )

    def finish_backward(h, pre):
        carry = (b_state * sr[1, h].astype(F32) + b_pre * pre.astype(F32)).astype(BF16)
        gk[:, cols(h)] = (att[:, cols(h)] + lmf[...] * nt(v[:, cols(h)], carry)).astype(BF16)
        gv[:, cols(h)] = (gvp[:, cols(h)] + lmf[...] * nn(k[:, cols(h)], carry)).astype(BF16)
        out_copy(1, gk, gk_hbm, h).start()
        out_copy(2, gv, gv_hbm, h).start()

    def backward_mine(i, x):
        finish_backward(mine + i, pf[1, i])
        return x

    lax.fori_loop(0, half, backward_mine, 0)

    def backward_other(c, x):
        state_copy(1, (1 - core) * C + c).wait_recv()
        final_copy(1, c).wait_recv()
        for u in range(CHUNK):
            finish_backward(other + c * CHUNK + u, pr[1, c * CHUNK + u])
        return x

    lax.fori_loop(0, C, backward_other, 0)

    for w in range(2):
        def drain(c, x, w=w):
            state_copy(w, c).wait_send()
            state_copy(w, C + c).wait_send()
            for j in range(J):
                step_copy(w, j, c).wait_send()
            final_copy(w, c).wait_send()
            return x

        lax.fori_loop(0, C, drain, 0)
    for j in range(len(gain_peers)):
        gain_copy(j).wait_send()
    out_lo.wait()

    def drain_out(h, x):
        out_copy(0, gq, gq_hbm, h).wait()
        out_copy(1, gk, gk_hbm, h).wait()
        out_copy(2, gv, gv_hbm, h).wait()
        return x

    lax.fori_loop(0, H, drain_out, 0)


def body(sizes, queries, keys, values, grad_out, doc_lengths, gain):
    n_dp, n_seq, n_tensor = sizes
    _, T, W = queries.shape
    H = W // HD
    half = H // 2
    C = half // CHUNK
    J = bits_of(n_seq) - 1
    docs = doc_lengths.shape[1]
    per = (3 + J) * C
    n_gain = bits_of(n_dp) + bits_of(n_seq)
    n_copy = 2 * per + bits_of(n_tensor) + n_gain
    big = jax.ShapeDtypeStruct((T, W), BF16)
    anywhere = pl.BlockSpec(memory_space=pl.ANY)
    vmem = pl.BlockSpec(memory_space=pltpu.VMEM)
    wide = pltpu.VMEM((T, W), BF16)
    wide32 = pltpu.VMEM((T, W), F32)
    column = pltpu.VMEM((T, HD), F32)
    column16 = pltpu.VMEM((T, HD), BF16)
    outs = pl.pallas_call(
        functools.partial(kernel, (n_dp, n_seq, n_tensor, docs)),
        out_shape=(big, big, big, big, jax.ShapeDtypeStruct((H, HD), F32)),
        in_specs=[pl.BlockSpec(memory_space=pltpu.SMEM)] + [anywhere] * 4 + [vmem],
        out_specs=[anywhere] * 4 + [vmem],
        scratch_shapes=[
            wide, wide, wide, wide,
            wide32, wide32,
            pltpu.VMEM((H, T, T), BF16),
            wide, wide, wide, wide, wide,
            pltpu.VMEM((T, T), F32),
            column, column, column16, column16,
            pltpu.VMEM((2, T, HD), F32),
            column, column,
            pltpu.VMEM((2, H, HD, HD), BF16),
            pltpu.VMEM((2, H, HD, HD), BF16),
            pltpu.VMEM((2, J, half, HD, HD), BF16),
            pltpu.VMEM((2, J, half, HD, HD), BF16),
            pltpu.VMEM((half, HD, HD), F32),
            pltpu.VMEM((2, half, HD, HD), BF16),
            pltpu.VMEM((2, half, HD, HD), BF16),
            pltpu.VMEM((H, HD, HD), BF16),
            pltpu.VMEM((bits_of(n_tensor), 8, T), F32),
            pltpu.VMEM((bits_of(n_tensor), 8, T), F32),
            pltpu.VMEM((n_gain, H, HD), F32),
            pltpu.VMEM((n_gain, H, HD), F32),
            pltpu.SemaphoreType.DMA((4,)),
            pltpu.SemaphoreType.DMA((3 * H + 1,)),
            pltpu.SemaphoreType.DMA((n_copy,)),
            pltpu.SemaphoreType.DMA((n_copy,)),
        ],
        compiler_params=pltpu.CompilerParams(
            collective_id=0, has_side_effects=True, vmem_limit_bytes=60 * 1024 * 1024
        ),
        cost_estimate=pl.CostEstimate(
            flops=16 * T * T * W, bytes_accessed=16 * T * W, transcendentals=0
        ),
    )(doc_lengths, queries[0], keys[0], values[0], grad_out[0], gain.reshape(H, HD))
    lo, gq, gk, gv, gg = outs
    return lo[None], gq[None], gk[None], gv[None], gg.reshape(W)


def solution(mesh):
    big = P("dp", "seq", "tensor")
    sizes = tuple(mesh.shape[axis] for axis in ("dp", "seq", "tensor"))
    return jax.shard_map(
        functools.partial(body, sizes),
        mesh=mesh,
        in_specs=(big, big, big, big, P("dp", None), P("tensor")),
        out_specs=(big, big, big, big, P("tensor")),
        check_vma=False,
    )
```

time: 193 us -> 78.1 us (0.40)
  Pallas kernels: 0 us -> 67.3 us
  matrix products: 48 us -> 0 us
  blocking collectives: 42.2 us -> 0 us
  local copies, waits for them, and re-layouts: 42.9 us -> 9.93 us
  other arithmetic: 25.2 us -> 0 us
  between operations: 17.8 us -> 0.66 us
  waiting for transfers between devices: 15.9 us -> 0 us
    pallas_call x0 -> x1, Pallas kernels: none -> 67.3 us  [body(): pl.pallas_call(functools.partial(kernel, (n_dp, n_seq, n_tensor, docs)),...]
    dot_general x12 -> x0, matrix products: 48 us -> none  [the longest x1 6.56 us: body(): jnp.einsum('hts,htd->hsd', d_scores, query, preferred_element_type=jnp.fl...]
    psum x3 -> x0, blocking collectives: 42.2 us -> none  [the longest x1 32.1 us: body(): grad_gain = lax.psum(jnp.sum(upstream * unit, axis=0), ('dp', 'seq'))]
    unnamed x32 -> x13, local copies, waits for them, and re-layouts: 27.3 us -> 9.93 us
    all_gather x2 -> x0, waiting for transfers between devices: 15.9 us -> none  [carried(): piece = lax.all_gather(state[None], 'seq', axis=0, tiled=True)]
    reduce_sum x5 -> x0, other arithmetic: 12.6 us -> none  [the longest x2 6.56 us: carried(): jnp.sum(jnp.where(keeping[:, None, None, None], piece.astype(jnp.float32)...]
    reshape x2 -> x0, local copies, waits for them, and re-layouts: 10.8 us -> none  [body(): attended = jnp.transpose(attended, (1, 0, 2)).reshape(count, local_width)]
    transpose x1 -> x0, other arithmetic: 4.25 us -> none  [head_major(): return jnp.transpose(array.reshape(shape), (1, 0, 2))]
  transfers between devices with their start and end apart: 2 -> 0, of which waited for: 1 -> 0; matrix products, arithmetic and copies ran while one was open for 27% -> 0% of each run, Pallas kernels for 0% -> 0%
where the time goes in v1:
time: 78.1 us; the launch traced here: 77.8 us
  Pallas kernels  67.3 us (86%)
  local copies, waits for them, and re-layouts  9.93 us (13%)
    pallas_call x1, Pallas kernels, body(): pl.pallas_call(functools.partial(kernel, (n_dp, n_seq, n_tensor, docs)),...  67.3 us
    unnamed x13, local copies, waits for them, and re-layouts  9.93 us

profile of v1, /device:TPU:0, one launch (start us, length us, event | category | flops | bytes accessed | tf_op | source)
XLA Modules:
  0.0 77.8 jit_solution(7626176415755610202)
XLA Ops:
  0.6 67.3 %shard_map.101 = (bf16[512,2048]{1,0:T(8,128)(2,1)}, bf16[512,2048]{1,0:T(8,128)(2,1)}, bf16[512,2048]{1,0:T(8,128)(2,1)}, bf16[512,2048]{1,0:T(8,128)(2,1)}, f32[16,128]{1,0:T(8,128)}) custom-call(s32[1,4]{1,0:T(1,128)} %len_ref.1, bf16[512,2048]{1,0:T(8,128)(2,1)} %bitcast.15, bf16[512,2048]{1,0:T(8,128)(2,1)} %bitcast.16, bf16[512,2048]{1,0:T(8,128)(2,1)} %bitcast.17, ...), custom_call_target="tpu_custom_call" | custom-call | flops 8589934592 | bytes 16777216 | tf_op jit(solution)/shard_map/pallas_call | solution.py:409
  67.9 0.0 copy-start.2
  67.9 3.3 %copy.16 = bf16[1,512,2048]{2,1,0:T(8,128)(2,1)} copy(bf16[1,512,2048]{2,1,0:T(8,128)(2,1)} %bitcast.13) | data formatting | bytes 4194304
  71.2 0.0 copy-done.2
  71.2 0.0 copy-start.1
  71.2 1.3 %copy.17 = bf16[1,512,2048]{2,1,0:T(8,128)(2,1)} copy(bf16[1,512,2048]{2,1,0:T(8,128)(2,1)S(1)} %bitcast.12) | data formatting | bytes 4194304
  72.5 1.0 %copy-done.1 = bf16[512,2048]{1,0:T(8,128)(2,1)S(1)} copy-done((bf16[512,2048]{1,0:T(8,128)(2,1)S(1)}, bf16[512,2048]{1,0:T(8,128)(2,1)}, u32[]{:S(2)}) %copy-start.1) | copy-done | bytes 2097176
  73.6 0.0 copy-start
  73.6 1.3 %copy.18 = bf16[1,512,2048]{2,1,0:T(8,128)(2,1)} copy(bf16[1,512,2048]{2,1,0:T(8,128)(2,1)S(1)} %bitcast.11) | data formatting | bytes 4194304
  74.9 1.0 %copy-done = bf16[512,2048]{1,0:T(8,128)(2,1)S(1)} copy-done((bf16[512,2048]{1,0:T(8,128)(2,1)S(1)}, bf16[512,2048]{1,0:T(8,128)(2,1)}, u32[]{:S(2)}) %copy-start) | copy-done | bytes 2097176
  75.9 0.0 copy-start.3
  75.9 1.3 %copy.19 = bf16[1,512,2048]{2,1,0:T(8,128)(2,1)} copy(bf16[1,512,2048]{2,1,0:T(8,128)(2,1)S(1)} %bitcast.10) | data formatting | bytes 4194304
  77.2 0.0 copy-done.3
  77.2 0.6 copy.20
Async XLA Ops:
  67.9 3.3 %copy-start.2 = (bf16[512,2048]{1,0:T(8,128)(2,1)S(1)}, bf16[512,2048]{1,0:T(8,128)(2,1)}, u32[]{:S(2)}) copy-start(bf16[512,2048]{1,0:T(8,128)(2,1)} %get-tuple-element.11) | copy-start | bytes 6291460
  71.2 2.3 %copy-start.1 = (bf16[512,2048]{1,0:T(8,128)(2,1)S(1)}, bf16[512,2048]{1,0:T(8,128)(2,1)}, u32[]{:S(2)}) copy-start(bf16[512,2048]{1,0:T(8,128)(2,1)} %get-tuple-element.12) | copy-start | bytes 6291460
  73.6 2.3 %copy-start = (bf16[512,2048]{1,0:T(8,128)(2,1)S(1)}, bf16[512,2048]{1,0:T(8,128)(2,1)}, u32[]{:S(2)}) copy-start(bf16[512,2048]{1,0:T(8,128)(2,1)} %get-tuple-element.13) | copy-start | bytes 6291460
  75.9 1.3 %copy-start.3 = (f32[16,128]{1,0:T(8,128)S(1)}, f32[16,128]{1,0:T(8,128)}, u32[]{:S(2)}) copy-start(f32[16,128]{1,0:T(8,128)} %get-tuple-element.14) | copy-start | bytes 24580

commit v2 on v1

--- a/solution.py
+++ b/solution.py
@@ -9,6 +9,7 @@
 
 HD = 128
 CHUNK = 2
+PAIR = 2
 EPSILON = 1e-05
 MESH = pl.DeviceIdType.MESH
 F32 = jnp.float32
@@ -28,7 +29,15 @@
 
 
 def cols(h):
-    return pl.ds(pl.multiple_of(h * HD, HD), HD)
+    return pl.ds(pl.multiple_of(h * HD, PAIR * HD), PAIR * HD)
+
+
+def parts(wide):
+    return [wide[:, u * HD:(u + 1) * HD] for u in range(PAIR)]
+
+
+def joined(pieces):
+    return jnp.concatenate(pieces, axis=1)
 
 
 def bits_of(n):
@@ -37,8 +46,8 @@
 
 def kernel(
     sizes, len_ref, q_hbm, k_hbm, v_hbm, g_hbm, gain_ref,
-    lo_hbm, gq_hbm, gk_hbm, gv_hbm, gg_ref,
-    q, k, v, g, att, gvp, scr, dat, lo, gq, gk, gv, mask, fmf, lmf, fmb, lmb,
+    lo_hbm, gq_hbm, gk_hbm, gv_hbm, gg_ref, cb, lmf,
+    q, k, v, g, att, scr, dat, lo, gq, gk, gv, mask, fmf, fmb, lmb,
     acc, rs, qs, st, sr, sa, rr, pacc, pf, pr, ci, ts, tr, gs, gr,
     in_sem, out_sem, ssem, rsem,
 ):
@@ -204,8 +213,9 @@
 
         def to(upto):
             nonlocal done
+            upto = upto // PAIR * PAIR
             if upto > done:
-                lax.fori_loop(done, upto, lambda h, x: (work(h), x)[1], 0)
+                lax.fori_loop(done // PAIR, upto // PAIR, lambda i, x: (work(i * PAIR), x)[1], 0)
                 done = upto
 
         to(before)
@@ -225,9 +235,11 @@
     pl.semaphore_wait(barrier, len(peers))
 
     def state_chunk(i, x):
-        for u in range(CHUNK):
-            h = lax.rem(other + i * CHUNK + u, H)
-            st[0, h] = tn(k[:, cols(h)] * lmb[...], v[:, cols(h)]).astype(BF16)
+        h = lax.rem(other + i * CHUNK, H)
+        ks, vs = parts(k[:, cols(h)]), parts(v[:, cols(h)])
+        new = [tn(kk * lmb[...], vv).astype(BF16) for kk, vv in zip(ks, vs)]
+        for u in range(PAIR):
+            st[0, h + u] = new[u]
         state_copy(0, lax.rem((1 - core) * C + i, 2 * C)).start()
         return x
 
@@ -235,37 +247,48 @@
     loads[2].wait()
 
     def local_forward(h):
-        qh, kh, vh = q[:, cols(h)], k[:, cols(h)], v[:, cols(h)]
-        top = (nt(qh[:T2], kh[:T2]) * mask[:T2, :T2]).astype(BF16)
-        low = (nt(qh[T2:], kh) * mask[T2:, :]).astype(BF16)
-        scr[h, :T2, :T2] = top
-        scr[h, T2:, :] = low
-        att[:T2, cols(h)] = nn(top, vh[:T2])
-        att[T2:, cols(h)] = nn(low, vh)
+        qs_, ks_, vs_ = parts(q[:, cols(h)]), parts(k[:, cols(h)]), parts(v[:, cols(h)])
+        top = [(nt(a[:T2], b[:T2]) * mask[:T2, :T2]).astype(BF16) for a, b in zip(qs_, ks_)]
+        low = [(nt(a[T2:], b) * mask[T2:, :]).astype(BF16) for a, b in zip(qs_, ks_)]
+        up = [nn(a, b[:T2]) for a, b in zip(top, vs_)]
+        down = [nn(a, b) for a, b in zip(low, vs_)]
+        for u in range(PAIR):
+            scr[h + u, :T2, :T2] = top[u]
+            scr[h + u, T2:, :] = low[u]
+        att[:T2, cols(h)] = joined(up)
+        att[T2:, cols(h)] = joined(down)
 
     interleave(0, fwd, local_forward, 2, [])
     loads[3].wait()
     acc[...] = jnp.zeros_like(acc)
 
     def finish_forward(h, pre):
-        carry = (f_state * sr[0, h].astype(F32) + f_pre * pre.astype(F32)).astype(BF16)
-        ci[h] = carry
-        x = att[:, cols(h)] + fmf[...] * nn(q[:, cols(h)], carry)
-        att[:, cols(h)] = x
-        acc[0] += x * x
-        acc[1] += (g[:, cols(h)].astype(F32) * gain_ref[pl.ds(h, 1), :]) * x
+        carry = [
+            (f_state * sr[0, h + u].astype(F32) + f_pre * pre[u].astype(F32)).astype(BF16)
+            for u in range(PAIR)
+        ]
+        old, up = parts(att[:, cols(h)]), parts(g[:, cols(h)])
+        query = parts(q[:, cols(h)])
+        gains = [gain_ref[pl.ds(h + u, 1), :] for u in range(PAIR)]
+        x = [old[u] + fmf[...] * nn(query[u], carry[u]) for u in range(PAIR)]
+        squares = sum(x[u] * x[u] for u in range(PAIR))
+        inners = sum((up[u].astype(F32) * gains[u]) * x[u] for u in range(PAIR))
+        acc[0] += squares
+        acc[1] += inners
+        for u in range(PAIR):
+            ci[h + u] = carry[u]
+        att[:, cols(h)] = joined(x)
 
     def forward_mine(i, x):
-        finish_forward(mine + i, pf[0, i])
-        return x
-
-    lax.fori_loop(0, half, forward_mine, 0)
+        finish_forward(mine + i * PAIR, [pf[0, i * PAIR + u] for u in range(PAIR)])
+        return x
+
+    lax.fori_loop(0, half // PAIR, forward_mine, 0)
 
     def forward_other(c, x):
         state_copy(0, (1 - core) * C + c).wait_recv()
         final_copy(0, c).wait_recv()
-        for u in range(CHUNK):
-            finish_forward(other + c * CHUNK + u, pr[0, c * CHUNK + u])
+        finish_forward(other + c * PAIR, [pr[0, c * PAIR + u] for u in range(PAIR)])
         return x
 
     lax.fori_loop(0, C, forward_other, 0)
@@ -287,17 +310,24 @@
     qs[...] = jnp.broadcast_to(rscale * rscale * inner, (HD, T)).T
 
     def back_chunk(i, x):
-        for u in range(CHUNK):
-            h = lax.rem(other + i * CHUNK + u, H)
-            a = att[:, cols(h)]
-            up = g[:, cols(h)].astype(F32)
-            gain = gain_ref[pl.ds(h, 1), :]
-            unit = a * rs[...]
-            lo[:, cols(h)] = (gain * unit).astype(BF16)
-            gs[0, pl.ds(h, 1), :] = jnp.sum(up * unit, axis=0, keepdims=True)
-            d = (rs[...] * (up * gain) - qs[...] * a).astype(BF16)
-            dat[:, cols(h)] = d
-            st[1, h] = tn(q[:, cols(h)] * fmb[...], d).astype(BF16)
+        h = lax.rem(other + i * CHUNK, H)
+        old = parts(att[:, cols(h)])
+        ups = [p.astype(F32) for p in parts(g[:, cols(h)])]
+        query = parts(q[:, cols(h)])
+        gains = [gain_ref[pl.ds(h + u, 1), :] for u in range(PAIR)]
+        unit = [old[u] * rs[...] for u in range(PAIR)]
+        out = [(gains[u] * unit[u]).astype(BF16) for u in range(PAIR)]
+        gsum = [jnp.sum(ups[u] * unit[u], axis=0, keepdims=True) for u in range(PAIR)]
+        d = [
+            (rs[...] * (ups[u] * gains[u]) - qs[...] * old[u]).astype(BF16)
+            for u in range(PAIR)
+        ]
+        new = [tn(query[u] * fmb[...], d[u]).astype(BF16) for u in range(PAIR)]
+        lo[:, cols(h)] = joined(out)
+        dat[:, cols(h)] = joined(d)
+        for u in range(PAIR):
+            gs[0, pl.ds(h + u, 1), :] = gsum[u]
+            st[1, h + u] = new[u]
         state_copy(1, lax.rem((1 - core) * C + i, 2 * C)).start()
         return x
 
@@ -325,18 +355,30 @@
         return pltpu.make_async_copy(src.at[:, cols(h)], dst.at[:, cols(h)], out_sem.at[n * H + h])
 
     def local_backward(h):
-        qh, kh, vh, dh = q[:, cols(h)], k[:, cols(h)], v[:, cols(h)], dat[:, cols(h)]
-        top = (nt(dh[:T2], vh[:T2]) * mask[:T2, :T2]).astype(BF16)
-        low = (nt(dh[T2:], vh) * mask[T2:, :]).astype(BF16)
-        into = nt(dh, ci[h]) * fmf[...]
-        gq[:T2, cols(h)] = (nn(top, kh[:T2]) + into[:T2]).astype(BF16)
-        gq[T2:, cols(h)] = (nn(low, kh) + into[T2:]).astype(BF16)
+        qs_, ks_, vs_ = parts(q[:, cols(h)]), parts(k[:, cols(h)]), parts(v[:, cols(h)])
+        ds_ = parts(dat[:, cols(h)])
+        two = range(PAIR)
+        stop = [scr[h + u, :T2, :T2] for u in two]
+        slow = [scr[h + u, T2:, :] for u in two]
+        carry = [ci[h + u] for u in two]
+        top = [(nt(ds_[u][:T2], vs_[u][:T2]) * mask[:T2, :T2]).astype(BF16) for u in two]
+        low = [(nt(ds_[u][T2:], vs_[u]) * mask[T2:, :]).astype(BF16) for u in two]
+        v_up = [tn(stop[u], ds_[u][:T2]) + tn(slow[u][:, :T2], ds_[u][T2:]) for u in two]
+        v_down = [tn(slow[u][:, T2:], ds_[u][T2:]) for u in two]
+        into = [nt(ds_[u], carry[u]) * fmf[...] for u in two]
+        q_up = [nn(top[u], ks_[u][:T2]) + into[u][:T2] for u in two]
+        q_down = [nn(low[u], ks_[u]) + into[u][T2:] for u in two]
+        k_up = [tn(top[u], qs_[u][:T2]) + tn(low[u][:, :T2], qs_[u][T2:]) for u in two]
+        k_down = [tn(low[u][:, T2:], qs_[u][T2:]) for u in two]
+        gv[:T2, cols(h)] = joined(v_up).astype(BF16)
+        gv[T2:, cols(h)] = joined(v_down).astype(BF16)
+        gq[:T2, cols(h)] = joined(q_up).astype(BF16)
+        gq[T2:, cols(h)] = joined(q_down).astype(BF16)
+        gk[:T2, cols(h)] = joined(k_up).astype(BF16)
+        gk[T2:, cols(h)] = joined(k_down).astype(BF16)
         out_copy(0, gq, gq_hbm, h).start()
-        att[:T2, cols(h)] = tn(top, qh[:T2]) + tn(low[:, :T2], qh[T2:])
-        att[T2:, cols(h)] = tn(low[:, T2:], qh[T2:])
-        stop, slow = scr[h, :T2, :T2], scr[h, T2:, :]
-        gvp[:T2, cols(h)] = tn(stop, dh[:T2]) + tn(slow[:, :T2], dh[T2:])
-        gvp[T2:, cols(h)] = tn(slow[:, T2:], dh[T2:])
+        out_copy(1, gk, gk_hbm, h).start()
+        out_copy(2, gv, gv_hbm, h).start()
 
     interleave(
         1, bwd, local_backward, 4,
@@ -344,23 +386,23 @@
     )
 
     def finish_backward(h, pre):
-        carry = (b_state * sr[1, h].astype(F32) + b_pre * pre.astype(F32)).astype(BF16)
-        gk[:, cols(h)] = (att[:, cols(h)] + lmf[...] * nt(v[:, cols(h)], carry)).astype(BF16)
-        gv[:, cols(h)] = (gvp[:, cols(h)] + lmf[...] * nn(k[:, cols(h)], carry)).astype(BF16)
-        out_copy(1, gk, gk_hbm, h).start()
-        out_copy(2, gv, gv_hbm, h).start()
+        carry = [
+            (b_state * sr[1, h + u].astype(F32) + b_pre * pre[u].astype(F32)).astype(BF16)
+            for u in range(PAIR)
+        ]
+        for u in range(PAIR):
+            cb[h + u] = carry[u]
 
     def backward_mine(i, x):
-        finish_backward(mine + i, pf[1, i])
-        return x
-
-    lax.fori_loop(0, half, backward_mine, 0)
+        finish_backward(mine + i * PAIR, [pf[1, i * PAIR + u] for u in range(PAIR)])
+        return x
+
+    lax.fori_loop(0, half // PAIR, backward_mine, 0)
 
     def backward_other(c, x):
         state_copy(1, (1 - core) * C + c).wait_recv()
         final_copy(1, c).wait_recv()
-        for u in range(CHUNK):
-            finish_backward(other + c * CHUNK + u, pr[1, c * CHUNK + u])
+        finish_backward(other + c * PAIR, [pr[1, c * PAIR + u] for u in range(PAIR)])
         return x
 
     lax.fori_loop(0, C, backward_other, 0)
@@ -379,13 +421,25 @@
         gain_copy(j).wait_send()
     out_lo.wait()
 
-    def drain_out(h, x):
+    def drain_out(i, x):
+        h = i * PAIR
         out_copy(0, gq, gq_hbm, h).wait()
         out_copy(1, gk, gk_hbm, h).wait()
         out_copy(2, gv, gv_hbm, h).wait()
         return x
 
-    lax.fori_loop(0, H, drain_out, 0)
+    lax.fori_loop(0, H // PAIR, drain_out, 0)
+
+
+def finish_kernel(lo_in, gq_in, gk_in, gv_in, k, v, cb, lm, gg_in, lo, gq, gk, gv, gg):
+    lo[...] = lo_in[...]
+    gq[...] = gq_in[...]
+    gg[...] = gg_in[...]
+    ks, vs = parts(k[...]), parts(v[...])
+    more_k = joined([lm[...] * nt(vs[u], cb[u]) for u in range(PAIR)])
+    more_v = joined([lm[...] * nn(ks[u], cb[u]) for u in range(PAIR)])
+    gk[...] = (gk_in[...].astype(F32) + more_k).astype(BF16)
+    gv[...] = (gv_in[...].astype(F32) + more_v).astype(BF16)
 
 
 def body(sizes, queries, keys, values, grad_out, doc_lengths, gain):
@@ -404,20 +458,24 @@
     vmem = pl.BlockSpec(memory_space=pltpu.VMEM)
     wide = pltpu.VMEM((T, W), BF16)
     wide32 = pltpu.VMEM((T, W), F32)
+    args = (queries[0], keys[0], values[0], grad_out[0], gain.reshape(H, HD))
+    sums = jax.ShapeDtypeStruct((H, HD), F32)
+    carries = jax.ShapeDtypeStruct((H, HD, HD), BF16)
+    rows = jax.ShapeDtypeStruct((T, HD), F32)
     column = pltpu.VMEM((T, HD), F32)
     column16 = pltpu.VMEM((T, HD), BF16)
     outs = pl.pallas_call(
         functools.partial(kernel, (n_dp, n_seq, n_tensor, docs)),
-        out_shape=(big, big, big, big, jax.ShapeDtypeStruct((H, HD), F32)),
+        out_shape=(big, big, big, big, sums, carries, rows),
         in_specs=[pl.BlockSpec(memory_space=pltpu.SMEM)] + [anywhere] * 4 + [vmem],
-        out_specs=[anywhere] * 4 + [vmem],
+        out_specs=[anywhere] * 4 + [vmem] * 3,
         scratch_shapes=[
             wide, wide, wide, wide,
-            wide32, wide32,
+            wide32,
             pltpu.VMEM((H, T, T), BF16),
             wide, wide, wide, wide, wide,
             pltpu.VMEM((T, T), F32),
-            column, column, column16, column16,
+            column, column16, column16,
             pltpu.VMEM((2, T, HD), F32),
             column, column,
             pltpu.VMEM((2, H, HD, HD), BF16),
@@ -443,8 +501,25 @@
         cost_estimate=pl.CostEstimate(
             flops=16 * T * T * W, bytes_accessed=16 * T * W, transcendentals=0
         ),
-    )(doc_lengths, queries[0], keys[0], values[0], grad_out[0], gain.reshape(H, HD))
-    lo, gq, gk, gv, gg = outs
+    )(doc_lengths, *args)
+    lo, gq, gk, gv, gg, cb, lm = outs
+    block = pl.BlockSpec((T, PAIR * HD), lambda i: (0, i))
+    whole = pl.BlockSpec((H, HD), lambda i: (0, 0))
+    lo, gq, gk, gv, gg = pl.pallas_call(
+        finish_kernel,
+        grid=(H // PAIR,),
+        out_shape=(big, big, big, big, sums),
+        in_specs=[block] * 6 + [
+            pl.BlockSpec((PAIR, HD, HD), lambda i: (i, 0, 0)),
+            pl.BlockSpec((T, HD), lambda i: (0, 0)),
+            whole,
+        ],
+        out_specs=[block] * 4 + [whole],
+        compiler_params=pltpu.CompilerParams(vmem_limit_bytes=60 * 1024 * 1024),
+        cost_estimate=pl.CostEstimate(
+            flops=4 * T * W * HD, bytes_accessed=20 * T * W, transcendentals=0
+        ),
+    )(lo, gq, gk, gv, keys[0], values[0], cb, lm, gg)
     return lo[None], gq[None], gk[None], gv[None], gg.reshape(W)
 
 

time: 78.1 us -> 75 us (0.960)
  local copies, waits for them, and re-layouts: 9.93 us -> 0 us
  Pallas kernels: 67.3 us -> 73.8 us
    pallas_call x0 -> x1, Pallas kernels: none -> 10.9 us  [body(): pl.pallas_call(finish_kernel, grid=(H // PAIR,), out_shape=(big, big, big...]
    unnamed x13 -> x0, local copies, waits for them, and re-layouts: 9.93 us -> none
    pallas_call x1, Pallas kernels: 67.3 us -> 63 us  [body(): pl.pallas_call(functools.partial(kernel, (n_dp, n_seq, n_tensor, docs)),...]
where the time goes in v2:
time: 75 us; the launch traced here: 74.6 us
  Pallas kernels  73.8 us (98%)
  between operations  0.8 us (1%)
    pallas_call x1, Pallas kernels, body(): pl.pallas_call(functools.partial(kernel, (n_dp, n_seq, n_tensor, docs)),...  63 us
    pallas_call x1, Pallas kernels, body(): pl.pallas_call(finish_kernel, grid=(H // PAIR,), out_shape=(big, big, big...  10.9 us

profile of v2, /device:TPU:0, one launch (start us, length us, event | category | flops | bytes accessed | tf_op | source)
XLA Modules:
  0.0 74.6 jit_solution(17187429151540088224)
XLA Ops:
  0.6 63.0 %shard_map.101 = (bf16[512,2048]{1,0:T(8,128)(2,1)}, bf16[512,2048]{1,0:T(8,128)(2,1)}, bf16[512,2048]{1,0:T(8,128)(2,1)}, bf16[512,2048]{1,0:T(8,128)(2,1)}, f3...) custom-call(s32[1,4]{1,0:T(1,128)} %len_ref.1, bf16[512,2048]{1,0:T(8,128)(2,1)} %bitcast.14, ...), custom_call_target="tpu_custom_call" | custom-call | flops 8589934592 | bytes 16777216 | tf_op jit(solution)/shard_map/pallas_call | solution.py:467
  63.6 10.9 %shard_map.102 = (bf16[512,2048]{1,0:T(8,128)(2,1)}, bf16[512,2048]{1,0:T(8,128)(2,1)}, bf16[512,2048]{1,0:T(8,128)(2,1)}, bf16[512,2048]{1,0:T(8,128)(2,1)}, f32[16,128]{1,0:T(8,128)}) custom-call(bf16[512,2048]{1,0:T(8,128)(2,1)} %get-tuple-element.17.lo_in, bf16[512,2048]{1,0:T(8,128)(2,1)} %get-tuple-element.18.gq_in, ...), custom_call_target="tpu_custom_call" | custom-call | flops 536870912 | bytes 20971520 | tf_op jit(solution)/shard_map/pallas_call | solution.py:508

commit v3 on v2

--- a/solution.py
+++ b/solution.py
@@ -47,7 +47,7 @@
 def kernel(
     sizes, len_ref, q_hbm, k_hbm, v_hbm, g_hbm, gain_ref,
     lo_hbm, gq_hbm, gk_hbm, gv_hbm, gg_ref, cb, lmf,
-    q, k, v, g, att, scr, dat, lo, gq, gk, gv, mask, fmf, fmb, lmb,
+    q, k, v, g, att, scr, dat, lo, gq, gk, gv, mask, maskt, fmf, fmb, lmb,
     acc, rs, qs, st, sr, sa, rr, pacc, pf, pr, ci, ts, tr, gs, gr,
     in_sem, out_sem, ssem, rsem,
 ):
@@ -66,8 +66,8 @@
         pltpu.make_async_copy(src, dst, in_sem.at[i])
         for i, (src, dst) in enumerate(((k_hbm, k), (v_hbm, v), (q_hbm, q), (g_hbm, g)))
     ]
-    for load in loads:
-        load.start()
+    loads[0].start()
+    loads[1].start()
 
     me = lax.axis_index("seq")
     dp = lax.axis_index("dp")
@@ -157,6 +157,11 @@
             t_start = jnp.maximum(t_start, jnp.where(t_pos >= s, s, 0))
         inside = (s_pos <= t_pos) & (s_pos >= t_start)
         mask[r * HD:(r + 1) * HD, :] = jnp.where(inside, 1.0, 0.0).astype(F32)
+        c_start = jnp.zeros((HD, T), jnp.int32)
+        for s in starts:
+            c_start = jnp.maximum(c_start, jnp.where(s_pos >= s, s, 0))
+        inside = (t_pos <= s_pos) & (t_pos >= c_start)
+        maskt[r * HD:(r + 1) * HD, :] = jnp.where(inside, 1.0, 0.0).astype(F32)
 
     def remote(src, dst, index, peer):
         return pltpu.make_async_remote_copy(
@@ -232,6 +237,8 @@
 
     loads[0].wait()
     loads[1].wait()
+    loads[2].start()
+    loads[3].start()
     pl.semaphore_wait(barrier, len(peers))
 
     def state_chunk(i, x):
@@ -252,9 +259,11 @@
         low = [(nt(a[T2:], b) * mask[T2:, :]).astype(BF16) for a, b in zip(qs_, ks_)]
         up = [nn(a, b[:T2]) for a, b in zip(top, vs_)]
         down = [nn(a, b) for a, b in zip(low, vs_)]
+        left = [(nt(a[:T2], b) * maskt[:T2, :]).astype(BF16) for a, b in zip(ks_, qs_)]
+        right = [(nt(a[T2:], b[T2:]) * maskt[T2:, T2:]).astype(BF16) for a, b in zip(ks_, qs_)]
         for u in range(PAIR):
-            scr[h + u, :T2, :T2] = top[u]
-            scr[h + u, T2:, :] = low[u]
+            scr[h + u, :T2, :] = left[u]
+            scr[h + u, T2:, T2:] = right[u]
         att[:T2, cols(h)] = joined(up)
         att[T2:, cols(h)] = joined(down)
 
@@ -358,18 +367,20 @@
         qs_, ks_, vs_ = parts(q[:, cols(h)]), parts(k[:, cols(h)]), parts(v[:, cols(h)])
         ds_ = parts(dat[:, cols(h)])
         two = range(PAIR)
-        stop = [scr[h + u, :T2, :T2] for u in two]
-        slow = [scr[h + u, T2:, :] for u in two]
+        s_left = [scr[h + u, :T2, :] for u in two]
+        s_right = [scr[h + u, T2:, T2:] for u in two]
         carry = [ci[h + u] for u in two]
         top = [(nt(ds_[u][:T2], vs_[u][:T2]) * mask[:T2, :T2]).astype(BF16) for u in two]
         low = [(nt(ds_[u][T2:], vs_[u]) * mask[T2:, :]).astype(BF16) for u in two]
-        v_up = [tn(stop[u], ds_[u][:T2]) + tn(slow[u][:, :T2], ds_[u][T2:]) for u in two]
-        v_down = [tn(slow[u][:, T2:], ds_[u][T2:]) for u in two]
+        left = [(nt(vs_[u][:T2], ds_[u]) * maskt[:T2, :]).astype(BF16) for u in two]
+        right = [(nt(vs_[u][T2:], ds_[u][T2:]) * maskt[T2:, T2:]).astype(BF16) for u in two]
+        v_up = [nn(s_left[u], ds_[u]) for u in two]
+        v_down = [nn(s_right[u], ds_[u][T2:]) for u in two]
         into = [nt(ds_[u], carry[u]) * fmf[...] for u in two]
         q_up = [nn(top[u], ks_[u][:T2]) + into[u][:T2] for u in two]
         q_down = [nn(low[u], ks_[u]) + into[u][T2:] for u in two]
-        k_up = [tn(top[u], qs_[u][:T2]) + tn(low[u][:, :T2], qs_[u][T2:]) for u in two]
-        k_down = [tn(low[u][:, T2:], qs_[u][T2:]) for u in two]
+        k_up = [nn(left[u], qs_[u]) for u in two]
+        k_down = [nn(right[u], qs_[u][T2:]) for u in two]
         gv[:T2, cols(h)] = joined(v_up).astype(BF16)
         gv[T2:, cols(h)] = joined(v_down).astype(BF16)
         gq[:T2, cols(h)] = joined(q_up).astype(BF16)
@@ -381,7 +392,7 @@
         out_copy(2, gv, gv_hbm, h).start()
 
     interleave(
-        1, bwd, local_backward, 4,
+        1, bwd, local_backward, 2,
         [functools.partial(gain_step, j) for j in range(len(gain_peers))],
     )
 
@@ -435,11 +446,12 @@
     lo[...] = lo_in[...]
     gq[...] = gq_in[...]
     gg[...] = gg_in[...]
-    ks, vs = parts(k[...]), parts(v[...])
-    more_k = joined([lm[...] * nt(vs[u], cb[u]) for u in range(PAIR)])
-    more_v = joined([lm[...] * nn(ks[u], cb[u]) for u in range(PAIR)])
-    gk[...] = (gk_in[...].astype(F32) + more_k).astype(BF16)
-    gv[...] = (gv_in[...].astype(F32) + more_v).astype(BF16)
+    for h in range(k.shape[1] // HD):
+        here = slice(h * HD, (h + 1) * HD)
+        more_k = lm[...] * nt(v[:, here], cb[h])
+        more_v = lm[...] * nn(k[:, here], cb[h])
+        gk[:, here] = (gk_in[:, here].astype(F32) + more_k).astype(BF16)
+        gv[:, here] = (gv_in[:, here].astype(F32) + more_v).astype(BF16)
 
 
 def body(sizes, queries, keys, values, grad_out, doc_lengths, gain):
@@ -475,6 +487,7 @@
             pltpu.VMEM((H, T, T), BF16),
             wide, wide, wide, wide, wide,
             pltpu.VMEM((T, T), F32),
+            pltpu.VMEM((T, T), F32),
             column, column16, column16,
             pltpu.VMEM((2, T, HD), F32),
             column, column,
@@ -503,15 +516,16 @@
         ),
     )(doc_lengths, *args)
     lo, gq, gk, gv, gg, cb, lm = outs
-    block = pl.BlockSpec((T, PAIR * HD), lambda i: (0, i))
+    step_rows = min(T, 128)
+    block = pl.BlockSpec((step_rows, W), lambda i: (i, 0))
     whole = pl.BlockSpec((H, HD), lambda i: (0, 0))
     lo, gq, gk, gv, gg = pl.pallas_call(
         finish_kernel,
-        grid=(H // PAIR,),
+        grid=(T // step_rows,),
         out_shape=(big, big, big, big, sums),
         in_specs=[block] * 6 + [
-            pl.BlockSpec((PAIR, HD, HD), lambda i: (i, 0, 0)),
-            pl.BlockSpec((T, HD), lambda i: (0, 0)),
+            pl.BlockSpec((H, HD, HD), lambda i: (0, 0, 0)),
+            pl.BlockSpec((step_rows, HD), lambda i: (i, 0)),
             whole,
         ],
         out_specs=[block] * 4 + [whole],

time: 75 us -> 74.9 us (level)
    pallas_call x1, Pallas kernels: 63 us -> 64.5 us  [body(): pl.pallas_call(functools.partial(kernel, (n_dp, n_seq, n_tensor, docs)),...]
    pallas_call x1, Pallas kernels: 10.9 us -> 9.34 us  [body(): pl.pallas_call(finish_kernel, grid=(T // step_rows,), out_shape=(big, big...]
where the time goes in v3:
time: 74.9 us; the launch traced here: 74.7 us
  Pallas kernels  73.9 us (99%)
  between operations  0.8 us (1%)
    pallas_call x1, Pallas kernels, body(): pl.pallas_call(functools.partial(kernel, (n_dp, n_seq, n_tensor, docs)),...  64.5 us
    pallas_call x1, Pallas kernels, body(): pl.pallas_call(finish_kernel, grid=(T // step_rows,), out_shape=(big, big...  9.34 us

profile of v3, /device:TPU:0, one launch (start us, length us, event | category | flops | bytes accessed | tf_op | source)
XLA Modules:
  0.0 74.7 jit_solution(5382255153578276209)
XLA Ops:
  0.6 64.5 %shard_map.101 = (bf16[512,2048]{1,0:T(8,128)(2,1)}, bf16[512,2048]{1,0:T(8,128)(2,1)}, bf16[512,2048]{1,0:T(8,128)(2,1)}, bf16[512,2048]{1,0:T(8,128)(2,1)}, f3...) custom-call(s32[1,4]{1,0:T(1,128)} %len_ref.1, bf16[512,2048]{1,0:T(8,128)(2,1)} %bitcast.14, ...), custom_call_target="tpu_custom_call" | custom-call | flops 8589934592 | bytes 16777216 | tf_op jit(solution)/shard_map/pallas_call | solution.py:479
  65.2 9.3 %shard_map.102 = (bf16[512,2048]{1,0:T(8,128)(2,1)}, bf16[512,2048]{1,0:T(8,128)(2,1)}, bf16[512,2048]{1,0:T(8,128)(2,1)}, bf16[512,2048]{1,0:T(8,128)(2,1)}, f32[16,128]{1,0:T(8,128)}) custom-call(bf16[512,2048]{1,0:T(8,128)(2,1)} %get-tuple-element.17.lo_in, bf16[512,2048]{1,0:T(8,128)(2,1)} %get-tuple-element.18.gq_in, ...), custom_call_target="tpu_custom_call" | custom-call | flops 536870912 | bytes 20971520 | tf_op jit(solution)/shard_map/pallas_call | solution.py:522

commit v4 on v2

--- a/solution.py
+++ b/solution.py
@@ -66,8 +66,8 @@
         pltpu.make_async_copy(src, dst, in_sem.at[i])
         for i, (src, dst) in enumerate(((k_hbm, k), (v_hbm, v), (q_hbm, q), (g_hbm, g)))
     ]
-    for load in loads:
-        load.start()
+    loads[0].start()
+    loads[1].start()
 
     me = lax.axis_index("seq")
     dp = lax.axis_index("dp")
@@ -202,13 +202,11 @@
             pf[w, chunk(c)] = total.astype(BF16)
             final_copy(w, c).start()
 
-    def interleave(w, coef, work, before, extra):
+    def interleave(w, coef, work, before, extra, after=None):
         order = sorted(
             [(c + j, -j, c) for j in range(J) for c in range(C)]
         )
-        events = [functools.partial(begin_step, w, coef, c) for c in range(C)]
-        first = len(events)
-        events += [functools.partial(step, w, coef, -mj, c) for _, mj, c in order]
+        events = [(functools.partial(step, w, coef, -mj, c), -mj, c) for _, mj, c in order]
         done = 0
 
         def to(upto):
@@ -218,13 +216,12 @@
                 lax.fori_loop(done // PAIR, upto // PAIR, lambda i, x: (work(i * PAIR), x)[1], 0)
                 done = upto
 
-        to(before)
-        later = len(events) - first
-        for i, event in enumerate(events):
-            if i >= first:
-                to(before + ((H - before) * (i - first + 1)) // later)
+        for i, (event, j, c) in enumerate(events):
+            to(before + ((H - before) * (i + 1)) // len(events))
             event()
-            if extra and i >= first and (i - first) % 2 == 1:
+            if j == J - 1 and after is not None:
+                after(c)
+            if extra and i % 2 == 1:
                 extra.pop(0)()
         to(H)
         while extra:
@@ -232,18 +229,29 @@
 
     loads[0].wait()
     loads[1].wait()
+    loads[2].start()
+    loads[3].start()
     pl.semaphore_wait(barrier, len(peers))
 
-    def state_chunk(i, x):
-        h = lax.rem(other + i * CHUNK, H)
+    def state_chunk(h):
         ks, vs = parts(k[:, cols(h)]), parts(v[:, cols(h)])
         new = [tn(kk * lmb[...], vv).astype(BF16) for kk, vv in zip(ks, vs)]
         for u in range(PAIR):
             st[0, h + u] = new[u]
-        state_copy(0, lax.rem((1 - core) * C + i, 2 * C)).start()
-        return x
-
-    lax.fori_loop(0, 2 * C, state_chunk, 0)
+
+    def state_other(i, x):
+        state_chunk(other + i * CHUNK)
+        state_copy(0, (1 - core) * C + i).start()
+        return x
+
+    def state_mine(i, x):
+        state_chunk(mine + i * CHUNK)
+        begin_step(0, fwd, i)
+        state_copy(0, core * C + i).start()
+        return x
+
+    lax.fori_loop(0, C, state_other, 0)
+    lax.fori_loop(0, C, state_mine, 0)
     loads[2].wait()
 
     def local_forward(h):
@@ -258,7 +266,6 @@
         att[:T2, cols(h)] = joined(up)
         att[T2:, cols(h)] = joined(down)
 
-    interleave(0, fwd, local_forward, 2, [])
     loads[3].wait()
     acc[...] = jnp.zeros_like(acc)
 
@@ -279,11 +286,12 @@
             ci[h + u] = carry[u]
         att[:, cols(h)] = joined(x)
 
-    def forward_mine(i, x):
-        finish_forward(mine + i * PAIR, [pf[0, i * PAIR + u] for u in range(PAIR)])
-        return x
-
-    lax.fori_loop(0, half // PAIR, forward_mine, 0)
+    def forward_mine(c):
+        finish_forward(mine + c * PAIR, [pf[0, c * PAIR + u] for u in range(PAIR)])
+
+    interleave(
+        0, fwd, lambda i: local_forward(lax.rem(mine + i, H)), 0, [], forward_mine
+    )
 
     def forward_other(c, x):
         state_copy(0, (1 - core) * C + c).wait_recv()
@@ -309,8 +317,7 @@
     rs[...] = jnp.broadcast_to(rscale, (HD, T)).T
     qs[...] = jnp.broadcast_to(rscale * rscale * inner, (HD, T)).T
 
-    def back_chunk(i, x):
-        h = lax.rem(other + i * CHUNK, H)
+    def back_chunk(h):
         old = parts(att[:, cols(h)])
         ups = [p.astype(F32) for p in parts(g[:, cols(h)])]
         query = parts(q[:, cols(h)])
@@ -328,10 +335,20 @@
         for u in range(PAIR):
             gs[0, pl.ds(h + u, 1), :] = gsum[u]
             st[1, h + u] = new[u]
-        state_copy(1, lax.rem((1 - core) * C + i, 2 * C)).start()
-        return x
-
-    lax.fori_loop(0, 2 * C, back_chunk, 0)
+
+    def back_other(i, x):
+        back_chunk(other + i * CHUNK)
+        state_copy(1, (1 - core) * C + i).start()
+        return x
+
+    def back_mine(i, x):
+        back_chunk(mine + i * CHUNK)
+        begin_step(1, bwd, i)
+        state_copy(1, core * C + i).start()
+        return x
+
+    lax.fori_loop(0, C, back_other, 0)
+    lax.fori_loop(0, C, back_mine, 0)
     out_lo = pltpu.make_async_copy(lo, lo_hbm, out_sem.at[3 * H])
     out_lo.start()
 
@@ -381,7 +398,7 @@
         out_copy(2, gv, gv_hbm, h).start()
 
     interleave(
-        1, bwd, local_backward, 4,
+        1, bwd, local_backward, 0,
         [functools.partial(gain_step, j) for j in range(len(gain_peers))],
     )
 
@@ -435,11 +452,12 @@
     lo[...] = lo_in[...]
     gq[...] = gq_in[...]
     gg[...] = gg_in[...]
-    ks, vs = parts(k[...]), parts(v[...])
-    more_k = joined([lm[...] * nt(vs[u], cb[u]) for u in range(PAIR)])
-    more_v = joined([lm[...] * nn(ks[u], cb[u]) for u in range(PAIR)])
-    gk[...] = (gk_in[...].astype(F32) + more_k).astype(BF16)
-    gv[...] = (gv_in[...].astype(F32) + more_v).astype(BF16)
+    for h in range(k.shape[1] // HD):
+        here = slice(h * HD, (h + 1) * HD)
+        more_k = lm[...] * nt(v[:, here], cb[h])
+        more_v = lm[...] * nn(k[:, here], cb[h])
+        gk[:, here] = (gk_in[:, here].astype(F32) + more_k).astype(BF16)
+        gv[:, here] = (gv_in[:, here].astype(F32) + more_v).astype(BF16)
 
 
 def body(sizes, queries, keys, values, grad_out, doc_lengths, gain):
@@ -496,26 +514,27 @@
             pltpu.SemaphoreType.DMA((n_copy,)),
         ],
         compiler_params=pltpu.CompilerParams(
-            collective_id=0, has_side_effects=True, vmem_limit_bytes=60 * 1024 * 1024
+            collective_id=0, has_side_effects=True, vmem_limit_bytes=43 * 1024 * 1024
         ),
         cost_estimate=pl.CostEstimate(
             flops=16 * T * T * W, bytes_accessed=16 * T * W, transcendentals=0
         ),
     )(doc_lengths, *args)
     lo, gq, gk, gv, gg, cb, lm = outs
-    block = pl.BlockSpec((T, PAIR * HD), lambda i: (0, i))
+    step_rows = min(T, 128)
+    block = pl.BlockSpec((step_rows, W), lambda i: (i, 0))
     whole = pl.BlockSpec((H, HD), lambda i: (0, 0))
     lo, gq, gk, gv, gg = pl.pallas_call(
         finish_kernel,
-        grid=(H // PAIR,),
+        grid=(T // step_rows,),
         out_shape=(big, big, big, big, sums),
         in_specs=[block] * 6 + [
-            pl.BlockSpec((PAIR, HD, HD), lambda i: (i, 0, 0)),
-            pl.BlockSpec((T, HD), lambda i: (0, 0)),
+            pl.BlockSpec((H, HD, HD), lambda i: (0, 0, 0)),
+            pl.BlockSpec((step_rows, HD), lambda i: (i, 0)),
             whole,
         ],
         out_specs=[block] * 4 + [whole],
-        compiler_params=pltpu.CompilerParams(vmem_limit_bytes=60 * 1024 * 1024),
+        compiler_params=pltpu.CompilerParams(vmem_limit_bytes=14 * 1024 * 1024),
         cost_estimate=pl.CostEstimate(
             flops=4 * T * W * HD, bytes_accessed=20 * T * W, transcendentals=0
         ),

time: 75 us -> 65.6 us (0.87)
  Pallas kernels: 73.8 us -> 61.8 us
  local copies, waits for them, and re-layouts: 0 us -> 2.94 us
    pallas_call x1, Pallas kernels: 10.9 us -> 4.55 us  [body(): pl.pallas_call(finish_kernel, grid=(T // step_rows,), out_shape=(big, big...]
    pallas_call x1, Pallas kernels: 63 us -> 57.2 us  [body(): pl.pallas_call(functools.partial(kernel, (n_dp, n_seq, n_tensor, docs)),...]
    unnamed x0 -> x10, local copies, waits for them, and re-layouts: none -> 2.94 us
where the time goes in v4:
time: 65.6 us; the launch traced here: 65.4 us
  Pallas kernels  61.8 us (94%)
  local copies, waits for them, and re-layouts  2.94 us (4%)
  between operations  0.67 us (1%)
    pallas_call x1, Pallas kernels, body(): pl.pallas_call(functools.partial(kernel, (n_dp, n_seq, n_tensor, docs)),...  57.2 us
    pallas_call x1, Pallas kernels, body(): pl.pallas_call(finish_kernel, grid=(T // step_rows,), out_shape=(big, big...  4.55 us
    unnamed x10, local copies, waits for them, and re-layouts  2.94 us

profile of v4, /device:TPU:0, one launch (start us, length us, event | category | flops | bytes accessed | tf_op | source)
XLA Modules:
  0.0 65.4 jit_solution(1193313268861208030)
XLA Ops:
  0.6 0.0 copy-start.2
  0.6 1.6 %copy-done.2 = bf16[1,512,2048]{2,1,0:T(8,128)(2,1)S(1)} copy-done((bf16[1,512,2048]{2,1,0:T(8,128)(2,1)S(1)}, bf16[1,512,2048]{2,1,0:T(8,128)(2,1)}, u32[]{:S(2)}) %copy-start.2) | copy-done | bytes 2097176
  2.2 0.0 copy-start.3
  2.2 0.7 %copy-done.3 = f32[2048]{0:T(1024)S(1)} copy-done((f32[2048]{0:T(1024)S(1)}, f32[2048]{0:T(1024)}, u32[]{:S(2)}) %copy-start.3) | copy-done | bytes 8216
  2.9 0.0 copy-start.4
  2.9 0.7 copy-done.4
  3.6 0.0 copy-start
  3.6 0.0 copy-start.1
  3.6 57.2 %shard_map.101 = (bf16[512,2048]{1,0:T(8,128)(2,1)S(1)}, bf16[512,2048]{1,0:T(8,128)(2,1)S(1)}, bf16[512,2048]{1,0:T(8,128)(2,1)S(1)}, bf16[512,2048]{1,0:T(8,12...) custom-call(s32[1,4]{1,0:T(1,128)S(1)} %copy-done.4, ...), custom_call_target="tpu_custom_call" | custom-call | flops 8589934592 | bytes 16777216 | tf_op jit(solution)/shard_map/pallas_call | solution.py:485
  60.8 0.0 copy-done
  60.8 0.0 copy-done.1
  60.8 4.5 %shard_map.102 = (bf16[512,2048]{1,0:T(8,128)(2,1)}, bf16[512,2048]{1,0:T(8,128)(2,1)}, bf16[512,2048]{1,0:T(8,128)(2,1)}, bf16[512,2048]{1,0:T(8,128)(2,1)}, f32[16,128]{1,0:T(8,128)}) custom-call(bf16[512,2048]{1,0:T(8,128)(2,1)S(1)} %get-tuple-element.17.lo_in, bf16[512,2048]{1,0:T(8,128)(2,1)S(1)} %get-tuple-element.18.gq_in, ...), custom_call_target="tpu_custom_call" | custom-call | flops 536870912 | bytes 20971520 | tf_op jit(solution)/shard_map/pallas_call | solution.py:527
Async XLA Ops:
  0.6 1.6 %copy-start.2 = (bf16[1,512,2048]{2,1,0:T(8,128)(2,1)S(1)}, bf16[1,512,2048]{2,1,0:T(8,128)(2,1)}, u32[]{:S(2)}) copy-start(bf16[1,512,2048]{2,1,0:T(8,128)(2,1)} %param.6) | copy-start | bytes 6291460
  2.2 0.7 %copy-start.3 = (f32[2048]{0:T(1024)S(1)}, f32[2048]{0:T(1024)}, u32[]{:S(2)}) copy-start(f32[2048]{0:T(1024)} %param.11) | copy-start | bytes 24580
  2.9 0.7 %copy-start.4 = (s32[1,4]{1,0:T(1,128)S(1)}, s32[1,4]{1,0:T(1,128)}, u32[]{:S(2)}) copy-start(s32[1,4]{1,0:T(1,128)} %len_ref.1) | copy-start | bytes 52
  3.6 57.2 %copy-start = (bf16[1,512,2048]{2,1,0:T(8,128)(2,1)S(1)}, bf16[1,512,2048]{2,1,0:T(8,128)(2,1)}, u32[]{:S(2)}) copy-start(bf16[1,512,2048]{2,1,0:T(8,128)(2,1)} %param.7) | copy-start | bytes 6291460
  3.6 57.2 %copy-start.1 = (bf16[1,512,2048]{2,1,0:T(8,128)(2,1)S(1)}, bf16[1,512,2048]{2,1,0:T(8,128)(2,1)}, u32[]{:S(2)}) copy-start(bf16[1,512,2048]{2,1,0:T(8,128)(2,1)} %param.8) | copy-start | bytes 6291460
